TPU v7x, 32 devices: a whole 2x2x4 slice. The times are simulated.
32 devices in a mesh: blk: 4 (over y, x), shard: 8 (over z, core).
Axes of the slice: x: 2, y: 2, z: 4, core: 2. Of those that a mesh axis runs over, the one named last changes fastest.
Arguments:
- table: bfloat16 [65536, 400], P(('blk', 'shard')), may hold values from -3 to 3
- relation: bfloat16 [1345, 400], replicated, may hold values from -3 to 3
- owners: int32 [32768, 2], P(('blk', 'shard')), may hold values from 0 to 7, all different within a row; in each aligned block of 1024 rows (0 to 1023, 1024 to 2047, ...) at most 512 rows name the same one
- rows: int32 [32768, 2], P(('blk', 'shard')), may hold values from 0 to 2047
- rel_ids: int32 [32768], P(('blk', 'shard')), may hold values from 0 to 1344
- span_ids: int32 [32], P(('blk', 'shard')), may hold values from 0 to 1
Outputs:
- entity_grad: float32 [65536, 400], P(('blk', 'shard'))
- relation_grad: float32 [1345, 400], replicated
Inputs may be any that keep to these rules, and one draw needn't show every extreme that they name: Among the 1024 edges of one device no owner index is named by more than 512 edge ends; an edge's source and target owners differ; ends address rows of the devices with the same blk index.
All inputs are finite; a program needn't handle non-finite values.
Results may differ from a plain program's by a relative error of at most 0.0016.
Values may be sent and summed in bfloat16 or wider, within the bound.
A program may use at most 128 MiB of HBM per device.

v0:
```python
import math

import jax
import jax.numpy as jnp
from jax import lax
from jax.sharding import PartitionSpec as P

NEG = 1024


def from_behind(value, axis, by):
    length = lax.axis_size(axis)
    return lax.ppermute(value, axis, [(i, (i + by) % length) for i in range(length)])


def score_span(query_bf, span, weight):
    neg_score = lax.dot_general(
        query_bf, span, (((1,), (1,)), ((), ())), preferred_element_type=jnp.float32
    )
    neg_grad = (weight * jax.nn.sigmoid(neg_score)).astype(jnp.bfloat16)
    query_part = jnp.dot(neg_grad, span, preferred_element_type=jnp.float32)
    span_part = lax.dot_general(
        neg_grad, query_bf, (((0,), (0,)), ((), ())), preferred_element_type=jnp.float32
    )
    return (query_part, span_part)


def shards(table, relation, owners, rows, rel_ids, span_ids):
    n_shard = lax.axis_size("shard")
    n_blk = lax.axis_size("blk")
    edges = owners.shape[0]
    rows_own = table.shape[0]
    width = table.shape[1]
    half = width // 2
    capacity = 4 * edges // n_shard
    negatives = NEG
    flat_owner = owners.reshape(-1)
    flat_row = rows.reshape(-1)
    onehot = (flat_owner[:, None] == jnp.arange(n_shard, dtype=jnp.int32)[None, :]).astype(
        jnp.int32
    )
    ranking = jnp.sum(jnp.cumsum(onehot, axis=0) * onehot, axis=1) - 1
    slots = flat_owner * capacity + ranking
    requests = (
        jnp.zeros((n_shard * capacity,), jnp.int32)
        .at[slots]
        .set(flat_row)
        .reshape(n_shard, capacity)
    )
    asked_rows = lax.all_to_all(requests, "shard", split_axis=0, concat_axis=0, tiled=True)
    fetched = lax.all_to_all(table[asked_rows], "shard", split_axis=0, concat_axis=0, tiled=True)
    gotten = fetched.reshape(n_shard * capacity, width)[slots].reshape(edges, 2, width)
    source = gotten[:, 0].astype(jnp.float32)
    target = gotten[:, 1].astype(jnp.float32)
    rel_rows = relation[rel_ids].astype(jnp.float32)
    s_re, s_im = (source[:, :half], source[:, half:])
    r_re, r_im = (rel_rows[:, :half], rel_rows[:, half:])
    query = jnp.concatenate([s_re * r_re - s_im * r_im, s_re * r_im + s_im * r_re], axis=1)
    pos_grad = jax.nn.sigmoid(jnp.sum(query * target, axis=1)) - 1.0
    query_bf = query.astype(jnp.bfloat16)
    weight = 1.0 / math.sqrt(n_blk * negatives)
    span_start = span_ids[0] * negatives
    span = lax.dynamic_slice_in_dim(table, span_start, negatives, 0)
    query_grad = pos_grad[:, None] * target
    carried = jnp.zeros((negatives, width), jnp.float32)
    for visit in range(n_blk):
        query_part, span_part = score_span(query_bf, span, weight)
        query_grad = query_grad + query_part
        carried = carried + span_part
        if visit + 1 < n_blk:
            span = from_behind(span, "blk", 1)
        carried = from_behind(carried, "blk", 1)
    q_re, q_im = (query_grad[:, :half], query_grad[:, half:])
    source_grad = jnp.concatenate([q_re * r_re + q_im * r_im, q_im * r_re - q_re * r_im], axis=1)
    rel_term = jnp.concatenate([q_re * s_re + q_im * s_im, q_im * s_re - q_re * s_im], axis=1)
    target_grad = pos_grad[:, None] * query
    local_relation = jnp.zeros((relation.shape[0], width), jnp.float32).at[rel_ids].add(rel_term)
    relation_grad = lax.psum(local_relation, ("blk", "shard"))
    end_grads = jnp.stack([source_grad, target_grad], axis=1).reshape(2 * edges, width)
    outgoing = jnp.zeros((n_shard * capacity, width), jnp.float32).at[slots].set(end_grads)
    arrived = lax.all_to_all(
        outgoing.reshape(n_shard, capacity, width), "shard", split_axis=0, concat_axis=0, tiled=True
    )
    entity_grad = (
        jnp.zeros((rows_own, width), jnp.float32)
        .at[asked_rows.reshape(-1)]
        .add(arrived.reshape(-1, width))
    )
    current = lax.dynamic_slice_in_dim(entity_grad, span_start, negatives, 0)
    entity_grad = lax.dynamic_update_slice_in_dim(entity_grad, current + carried, span_start, 0)
    return (entity_grad, relation_grad)


def solution(mesh):
    in_specs = (
        P(("blk", "shard"), None),
        P(),
        P(("blk", "shard"), None),
        P(("blk", "shard"), None),
        P(("blk", "shard")),
        P(("blk", "shard")),
    )
    out_specs = (P(("blk", "shard"), None), P())
    return jax.shard_map(shards, mesh=mesh, in_specs=in_specs, out_specs=out_specs, check_vma=False)
```

profile of v0, /device:TPU:9, one launch (start us, length us, event | category | flops | bytes accessed | tf_op | source)
XLA Modules:
  0.0 565.6 jit_solution(10035841199535443975)
XLA Ops:
  13.3 8.6 %scatter_custom_fusion = s32[4096]{0:T(1024)} fusion(s32[2048]{0:T(1024)S(1)} %bitcast.73, s32[2048]{0:T(1024)S(1)} %reshape.235, s32[]{:T(128)} %constant.12.clone.1), kind=kCustom, calls=%fused_computation.51 | custom fusion | bytes 16388 | tf_op jit(solution)/shard_map/scatter | solution.py:47
  22.0 5.6 all-to-all-start
  31.5 17.3 %gather_fusion = bf16[4096,400]{1,0:T(8,128)(2,1)} fusion(bf16[2048,400]{1,0:T(8,128)(2,1)S(1)} %copy.48, s32[4096]{0:T(1024)S(1)} %broadcast_clamp_fusion), kind=kCustom, calls=%fused_computation | custom fusion | bytes 6569984 | tf_op jit(solution)/shard_map/gather | solution.py:51
  48.8 6.2 %copy.49 = bf16[8,512,400]{1,2,0:T(8,128)(2,1)} copy(bf16[8,512,400]{2,1,0:T(8,128)(2,1)} %bitcast.67) | data formatting | bytes 6553600 | tf_op jit(solution)/shard_map/gather | solution.py:51
  55.0 6.3 %all-to-all-start.1 = ((bf16[8,512,400]{1,2,0:T(8,128)(2,1)}), bf16[8,512,400]{1,2,0:T(8,128)(2,1)}, u32[]{:S(2)}, u32[]{:S(2)}) async-start(bf16[8,512,400]{1,2,0:T(8,128)(2,1)} %copy.49), calls=%async_computation.1 | async-start | bytes 6553600 | tf_op jit(solution)/shard_map/all_to_all | solution.py:51
  63.4 19.3 %collective-permute-done = bf16[1024,400]{0,1:T(8,128)(2,1)} collective-permute-done((bf16[1024,400]{0,1:T(8,128)(2,1)S(1)}, bf16[1024,400]{0,1:T(8,128)(2,1)}, u32[]{:S(2)}, u32[]{:S(2)}) %collective-permute-start) | collective-permute-done | bytes 819232 | tf_op jit(solution)/shard_map/ppermute | solution.py:13
  89.8 12.6 %collective-permute-done.1 = bf16[1024,400]{0,1:T(8,128)(2,1)} collective-permute-done((bf16[1024,400]{0,1:T(8,128)(2,1)}, bf16[1024,400]{0,1:T(8,128)(2,1)}, u32[]{:S(2)}, u32[]{:S(2)}) %collective-permute-start.1) | collective-permute-done | bytes 819232 | tf_op jit(solution)/shard_map/ppermute | solution.py:13
  102.4 29.6 %all-to-all-done.1 = bf16[8,512,400]{1,2,0:T(8,128)(2,1)} async-done(((bf16[8,512,400]{1,2,0:T(8,128)(2,1)}), bf16[8,512,400]{1,2,0:T(8,128)(2,1)}, u32[]{:S(2)}, u32[]{:S(2)}) %all-to-all-start.1) | async-done | bytes 3276832 | tf_op jit(solution)/shard_map/all_to_all | solution.py:51
  132.1 6.2 %copy.50 = bf16[8,512,400]{2,1,0:T(8,128)(2,1)} copy(bf16[8,512,400]{1,2,0:T(8,128)(2,1)} %all-to-all-done.1) | data formatting | bytes 6553600 | tf_op jit(solution)/shard_map/all_to_all | solution.py:51
  138.3 12.0 %gather_fusion.1 = bf16[2048,400]{1,0:T(8,128)(2,1)} fusion(bf16[4096,400]{1,0:T(8,128)(2,1)} %bitcast.65, s32[2048]{0:T(1024)S(1)} %broadcast_clamp_fusion.1), kind=kCustom, calls=%fused_computation.1 | custom fusion | bytes 3284992 | tf_op jit(solution)/shard_map/gather | solution.py:52
  157.2 4.6 copy.67
  161.9 4.9 copy.66
  197.4 6.2 %reshape.243 = f32[2048,400]{1,0:T(8,128)} reshape(f32[1024,2,400]{2,1,0:T(2,128)} %copy.55) | data formatting | bytes 6553600 | tf_op jit(solution)/shard_map/reshape | solution.py:79
  203.6 13.4 %scatter_custom_fusion.1 = f32[4096,400]{1,0:T(8,128)} fusion(s32[2048]{0:T(1024)S(1)} %bitcast.75, f32[2048,400]{1,0:T(8,128)} %reshape.243, f32[]{:T(128)} %constant.11.clone.1), kind=kCustom, calls=%fused_computation.11 | custom fusion | bytes 6554112 | tf_op jit(solution)/shard_map/scatter | solution.py:80
  217.0 8.5 %copy.56 = f32[8,512,400]{1,2,0:T(8,128)} copy(f32[8,512,400]{2,1,0:T(8,128)} %bitcast.66) | data formatting | bytes 13107200 | tf_op jit(solution)/shard_map/reshape | solution.py:82
  225.4 8.7 %all-to-all-start.2 = ((f32[8,512,400]{1,2,0:T(8,128)}), f32[8,512,400]{1,2,0:T(8,128)}, u32[]{:S(2)}, u32[]{:S(2)}) async-start(f32[8,512,400]{1,2,0:T(8,128)} %copy.56), calls=%async_computation.2 | async-start | bytes 13107200 | tf_op jit(solution)/shard_map/all_to_all | solution.py:81
  236.4 36.7 %collective-permute-done.3 = f32[1024,400]{0,1:T(8,128)S(1)} collective-permute-done((f32[1024,400]{0,1:T(8,128)S(1)}, f32[1024,400]{0,1:T(8,128)S(1)}, u32[]{:S(2)}, u32[]{:S(2)}) %collective-permute-start.3) | collective-permute-done | bytes 1638432 | tf_op jit(solution)/shard_map/ppermute | solution.py:13
  275.7 35.6 %collective-permute-done.4 = f32[1024,400]{0,1:T(8,128)S(1)} collective-permute-done((f32[1024,400]{0,1:T(8,128)S(1)}, f32[1024,400]{0,1:T(8,128)S(1)}, u32[]{:S(2)}, u32[]{:S(2)}) %collective-permute-start.4) | collective-permute-done | bytes 1638432 | tf_op jit(solution)/shard_map/ppermute | solution.py:13
  312.7 35.0 %collective-permute-done.5 = f32[1024,400]{0,1:T(8,128)S(1)} collective-permute-done((f32[1024,400]{0,1:T(8,128)S(1)}, f32[1024,400]{0,1:T(8,128)S(1)}, u32[]{:S(2)}, u32[]{:S(2)}) %collective-permute-start.5) | collective-permute-done | bytes 1638432 | tf_op jit(solution)/shard_map/ppermute | solution.py:13
  351.4 8.9 %scatter_custom_fusion.3 = f32[1345,400]{1,0:T(8,128)} fusion(s32[1024]{0:T(1024)S(1)} %get-tuple-element.18, f32[1024,400]{1,0:T(8,128)} %copy.61, f32[]{:T(128)} %constant.11.clone.1), kind=kCustom, calls=%fused_computation.28 | custom fusion | flops 409600 | bytes 2152512 | tf_op jit(solution)/shard_map/scatter-add | solution.py:77
  360.4 140.3 %all-reduce.2.cloned.1.call-done = f32[1345,400]{1,0:T(8,128)} async-done(((f32[1345,400]{1,0:T(8,128)}), f32[1345,400]{1,0:T(8,128)}) %all-reduce.2.cloned.1.call-update) | async-done | bytes 2152016 | tf_op jit(solution)/shard_map/psum | solution.py:78
  503.9 8.5 %copy.64 = f32[8,512,400]{2,1,0:T(8,128)} copy(f32[8,512,400]{1,2,0:T(8,128)} %all-to-all-done.2) | data formatting | bytes 13107200 | tf_op jit(solution)/shard_map/reshape | solution.py:87
  512.4 30.4 %scatter_custom_fusion.2 = f32[2048,400]{1,0:T(8,128)} fusion(s32[4096]{0:T(1024)S(1)} %bitcast.78, f32[4096,400]{1,0:T(8,128)} %bitcast.70, f32[]{:T(128)} %constant.11.clone.1), kind=kCustom, calls=%fused_computation.14 | custom fusion | flops 1638400 | bytes 3277312 | tf_op jit(solution)/shard_map/scatter-add | solution.py:87
  553.1 5.2 copy.62
  (112 shorter events, 79.2 us)
Async XLA Ops:
  22.0 9.5 %all-to-all-start = ((s32[8,1,512]{2,1,0:T(1,128)}), s32[8,1,512]{2,1,0:T(1,128)S(1)}, u32[]{:S(2)}, u32[]{:S(2)}) async-start(s32[8,1,512]{2,1,0:T(1,128)} %bitcast.3), calls=%async_computation | async-start | bytes 32768 | tf_op jit(solution)/shard_map/all_to_all | solution.py:50
  55.0 7.0 %copy-start.1 = (bf16[2048,400]{0,1:T(8,128)(2,1)S(1)}, bf16[2048,400]{0,1:T(8,128)(2,1)}, u32[]{:S(2)}) copy-start(bf16[2048,400]{0,1:T(8,128)(2,1)} %param.6) | copy-start | bytes 4915204
  55.0 77.1 %all-to-all-start.1 = ((bf16[8,512,400]{1,2,0:T(8,128)(2,1)}), bf16[8,512,400]{1,2,0:T(8,128)(2,1)}, u32[]{:S(2)}, u32[]{:S(2)}) async-start(bf16[8,512,400]{1,2,0:T(8,128)(2,1)} %copy.49), calls=%async_computation.1 | async-start | bytes 6553600 | tf_op jit(solution)/shard_map/all_to_all | solution.py:51
  61.3 21.7 %copy-start.6 = (bf16[1345,400]{0,1:T(8,128)(2,1)S(1)}, bf16[1345,400]{0,1:T(8,128)(2,1)}, u32[]{:S(2)}) copy-start(bf16[1345,400]{0,1:T(8,128)(2,1)} %param.7) | copy-start | bytes 3228004
  61.3 22.6 %copy-start.12 = (s32[1024]{0:T(1024)S(1)}, s32[1024]{0:T(1024)}, u32[]{:S(2)}) copy-start(s32[1024]{0:T(1024)} %param.10) | copy-start | bytes 12292
  62.1 20.5 %copy-start.9 = (bf16[1024,400]{0,1:T(8,128)(2,1)}, bf16[1024,400]{0,1:T(8,128)(2,1)S(1)}, u32[]{:S(2)}) copy-start(bf16[1024,400]{0,1:T(8,128)(2,1)S(1)} %constant_dynamic-slice_fusion.1) | copy-start | bytes 2457604
  62.1 20.5 %collective-permute-start = (bf16[1024,400]{0,1:T(8,128)(2,1)S(1)}, bf16[1024,400]{0,1:T(8,128)(2,1)}, u32[]{:S(2)}, u32[]{:S(2)}) collective-permute-start(bf16[1024,400]{0,1:T(8,128)(2,1)S(1)} %constant_dynamic-slice_fusion.1), channel_id=1, source_target_pairs={{0,8},{8,16},{16,24},{24,0},{1,9},{9,17},{17,25},{25,1},{2,10},{10... | collective-permute-start | bytes 2457608 | tf_op jit(solution)/shard_map/ppermute | solution.py:13
  82.7 19.8 %collective-permute-start.1 = (bf16[1024,400]{0,1:T(8,128)(2,1)}, bf16[1024,400]{0,1:T(8,128)(2,1)}, u32[]{:S(2)}, u32[]{:S(2)}) collective-permute-start(bf16[1024,400]{0,1:T(8,128)(2,1)} %collective-permute-done), channel_id=1, source_target_pairs={{0,8},{8,16},{16,24},{24,0},{1,9},{9,17},{17,25},{25,1},{2,10},{10... | collective-permute-start | bytes 2457608 | tf_op jit(solution)/shard_map/ppermute | solution.py:13
  102.4 76.4 %collective-permute-start.2 = (bf16[1024,400]{0,1:T(8,128)(2,1)}, bf16[1024,400]{0,1:T(8,128)(2,1)}, u32[]{:S(2)}, u32[]{:S(2)}) collective-permute-start(bf16[1024,400]{0,1:T(8,128)(2,1)} %collective-permute-done.1), channel_id=1, source_target_pairs={{0,8},{8,16},{16,24},{24,0},{1,9},{9,17},{17,25},{25,1},{2,10},{10... | collective-permute-start | bytes 2457608 | tf_op jit(solution)/shard_map/ppermute | solution.py:13
  167.6 11.3 %copy-start.7 = (bf16[1024,400]{0,1:T(8,128)(2,1)}, bf16[1024,400]{0,1:T(8,128)(2,1)S(1)}, u32[]{:S(2)}) copy-start(bf16[1024,400]{0,1:T(8,128)(2,1)S(1)} %fusion.11) | copy-start | bytes 2457604
  175.2 7.4 %copy-start.15 = (bf16[1024,1024]{1,0:T(8,128)(2,1)}, bf16[1024,1024]{1,0:T(8,128)(2,1)S(1)}, u32[]{:S(2)}) copy-start(bf16[1024,1024]{1,0:T(8,128)(2,1)S(1)} %multiply_convert_fusion.1) | copy-start | bytes 6291460
  225.4 8.7 %copy-start.8 = (bf16[1024,400]{0,1:T(8,128)(2,1)S(1)}, bf16[1024,400]{0,1:T(8,128)(2,1)}, u32[]{:S(2)}) copy-start(bf16[1024,400]{0,1:T(8,128)(2,1)} %copy-done.7) | copy-start | bytes 2457604
  225.4 8.7 %copy-start.18 = (bf16[1024,1024]{1,0:T(8,128)(2,1)S(1)}, bf16[1024,1024]{1,0:T(8,128)(2,1)}, u32[]{:S(2)}) copy-start(bf16[1024,1024]{1,0:T(8,128)(2,1)} %copy-done.17) | copy-start | bytes 6291460
  225.4 278.4 %all-to-all-start.2 = ((f32[8,512,400]{1,2,0:T(8,128)}), f32[8,512,400]{1,2,0:T(8,128)}, u32[]{:S(2)}, u32[]{:S(2)}) async-start(f32[8,512,400]{1,2,0:T(8,128)} %copy.56), calls=%async_computation.2 | async-start | bytes 13107200 | tf_op jit(solution)/shard_map/all_to_all | solution.py:81
  234.1 266.5 %all-reduce.2.cloned.1.call-start = ((), (), s32[]{:S(2)}) async-start(), calls=%async_computation.3 | async-start | bytes 5537792 | tf_op jit(solution)/shard_map/psum | solution.py:78
  234.2 39.0 %copy-start.14 = (bf16[1024,1024]{1,0:T(8,128)(2,1)S(1)}, bf16[1024,1024]{1,0:T(8,128)(2,1)}, u32[]{:S(2)}) copy-start(bf16[1024,1024]{1,0:T(8,128)(2,1)} %copy-done.13) | copy-start | bytes 6291460
  235.2 39.5 %copy-start.16 = (bf16[1024,1024]{1,0:T(8,128)(2,1)S(1)}, bf16[1024,1024]{1,0:T(8,128)(2,1)}, u32[]{:S(2)}) copy-start(bf16[1024,1024]{1,0:T(8,128)(2,1)} %copy-done.15) | copy-start | bytes 6291460
  235.2 38.0 %collective-permute-start.3 = (f32[1024,400]{0,1:T(8,128)S(1)}, f32[1024,400]{0,1:T(8,128)S(1)}, u32[]{:S(2)}, u32[]{:S(2)}) collective-permute-start(f32[1024,400]{0,1:T(8,128)S(1)} %fusion.21), channel_id=1, source_target_pairs={{0,8},{8,16},{16,24},{24,0},{1,9},{9,17},{17,25},{25,1},{2,10},{10... | collective-permute-start | bytes 4915208 | tf_op jit(solution)/shard_map/ppermute | solution.py:13
  274.2 37.1 %collective-permute-start.4 = (f32[1024,400]{0,1:T(8,128)S(1)}, f32[1024,400]{0,1:T(8,128)S(1)}, u32[]{:S(2)}, u32[]{:S(2)}) collective-permute-start(f32[1024,400]{0,1:T(8,128)S(1)} %convolution_add_fusion), channel_id=1, source_target_pairs={{0,8},{8,16},{16,24},{24,0},{1,9},{9,17},{17,25},{25,1},{2,10},{10... | collective-permute-start | bytes 4915208 | tf_op jit(solution)/shard_map/ppermute | solution.py:13
  275.7 36.0 %copy-start.5 = (bf16[1024,1024]{1,0:T(8,128)(2,1)S(1)}, bf16[1024,1024]{1,0:T(8,128)(2,1)}, u32[]{:S(2)}) copy-start(bf16[1024,1024]{1,0:T(8,128)(2,1)} %copy-done.4) | copy-start | bytes 6291460
  311.6 36.1 %collective-permute-start.5 = (f32[1024,400]{0,1:T(8,128)S(1)}, f32[1024,400]{0,1:T(8,128)S(1)}, u32[]{:S(2)}, u32[]{:S(2)}) collective-permute-start(f32[1024,400]{0,1:T(8,128)S(1)} %add.149), channel_id=1, source_target_pairs={{0,8},{8,16},{16,24},{24,0},{1,9},{9,17},{17,25},{25,1},{2,10},{10... | collective-permute-start | bytes 4915208 | tf_op jit(solution)/shard_map/ppermute | solution.py:13
  312.7 36.5 %copy-start.2 = (f32[1024,200]{0,1:T(8,128)S(1)}, f32[1024,200]{0,1:T(8,128)}, u32[]{:S(2)}) copy-start(f32[1024,200]{0,1:T(8,128)} %get-tuple-element.8) | copy-start | bytes 2457604
  312.7 36.5 %copy-start.3 = (f32[1024,200]{0,1:T(8,128)S(1)}, f32[1024,200]{0,1:T(8,128)}, u32[]{:S(2)}) copy-start(f32[1024,200]{0,1:T(8,128)} %get-tuple-element.9) | copy-start | bytes 2457604
  349.2 197.0 %collective-permute-start.6 = (f32[1024,400]{0,1:T(8,128)}, f32[1024,400]{0,1:T(8,128)}, u32[]{:S(2)}, u32[]{:S(2)}) collective-permute-start(f32[1024,400]{0,1:T(8,128)} %add.150), channel_id=1, source_target_pairs={{0,8},{8,16},{16,24},{24,0},{1,9},{9,17},{17,25},{25,1},{2,10},{10... | collective-permute-start | bytes 4915208 | tf_op jit(solution)/shard_map/ppermute | solution.py:13
  (6 other events, 25.0 us)
Sparse Core Ops, SparseCore 0:
  360.5 140.1 all-reduce.1
where the time goes:
time: 577 us; the launch traced here: 566 us
  waiting for transfers between devices  310 us (54%)
  local copies, waits for them, and re-layouts  137 us (24%)
  other arithmetic  53.5 us (9%)
  matrix products  24.7 us (4%)
  starting transfers between devices  24 us (4%)
  between operations  15.8 us (3%)
    psum x1, waiting for transfers between devices, shards(): relation_grad = lax.psum(local_relation, ('blk', 'shard'))  140 us
    ppermute x7, waiting for transfers between devices, from_behind(): lax.ppermute(value, axis, [(i, (i + by) % length) for i in range(length)])  139 us
    scatter-add x1, other arithmetic, shards(): entity_grad = jnp.zeros((rows_own, width), jnp.float32).at[asked_rows.res...  30.4 us
    all_to_all x1, waiting for transfers between devices, shards(): lax.all_to_all(table[asked_rows], 'shard', split_axis=0, concat_axis=0, t...  29.6 us
    unnamed x47, local copies, waits for them, and re-layouts  25.7 us
    gather x2, local copies, waits for them, and re-layouts, shards(): table[asked_rows]  23.5 us
    scatter x1, local copies, waits for them, and re-layouts, shards(): jnp.zeros((n_shard * capacity, width), jnp.float32).at[slots].set(end_grads)  13.4 us
    dot_general x4, matrix products, score_span(): lax.dot_general(query_bf, span, (((1,), (1,)), ((), ())), preferred_eleme...  12.3 us
  transfers between devices with their start and end apart: 11, of which 8 were waited for; matrix products, arithmetic and copies ran while one was open for 21% of the time, Pallas kernels for 0%

commit v1 on v0

v1 whole, which is shorter than its diff:
```python
import functools
import math

import jax
import jax.numpy as jnp
from jax import lax
from jax.experimental import pallas as pl
from jax.experimental.pallas import tpu as pltpu
from jax.sharding import PartitionSpec as P

NEG = 1024
F32 = jnp.float32
BF = jnp.bfloat16
MESH = pl.DeviceIdType.MESH
NN = (((1,), (0,)), ((), ()))
NT = (((1,), (1,)), ((), ()))
TN = (((0,), (0,)), ((), ()))


def dot(a, b, dims):
    return lax.dot_general(a, b, dims, preferred_element_type=F32)


def onehot(count, first, ids):
    at = lax.broadcasted_iota(jnp.int32, (count, ids.shape[1]), 0) + first
    return jnp.where(at == ids, 1.0, 0.0).astype(BF)


def kernel(
    n, nb, cap, piece,
    table, relation, slots, wanted, rel_ids, span_id,
    entity, relation_out,
    req_out, req_in, row_out, row_in, grad_in,
    spans, back_out, back_in, own_back,
    rel_pad, rel_rows, query_s, query_bf, query_grad, end_grads, rel_lo,
    r1_out, r1_in, r2_out, r2_in, r3, r4_in,
    req_ss, req_rs, row_ss, row_rs, grad_ss, grad_rs,
    span_ss, span_rs, back_ss, back_rs, r1_ss, r1_rs, r2_ss, r2_rs, r3_ss, r3_rs, r4_ss, r4_rs,
):
    width, own_rows = table.shape
    half = width // 2
    edges = rel_ids.shape[1]
    types = relation.shape[1]
    part = r3.shape[1]
    negatives = spans.shape[2]
    weight = 1.0 / math.sqrt(nb * negatives)
    ends, rel_hi, grad_out = entity, query_bf, row_out
    chunk = 512
    me, mb = lax.axis_index("shard"), lax.axis_index("blk")

    barrier = pltpu.get_barrier_semaphore()

    def greet(i, _):
        pl.semaphore_signal(
            barrier, inc=1, device_id={"shard": lax.rem(me + i, n)}, device_id_type=MESH
        )
        return 0

    lax.fori_loop(1, n, greet, 0)
    for i in range(1, nb):
        pl.semaphore_signal(
            barrier, inc=1, device_id={"blk": lax.rem(mb + i, nb)}, device_id_type=MESH
        )
    pl.semaphore_wait(barrier, n + nb - 2)

    def to_shard(src, dst, ss, rs, to, frm):
        return pltpu.make_async_remote_copy(
            src_ref=src, dst_ref=dst, send_sem=ss.at[to], recv_sem=rs.at[frm],
            device_id={"shard": to}, device_id_type=MESH,
        )

    def to_blk(src, dst, ss, rs, to, frm):
        return pltpu.make_async_remote_copy(
            src_ref=src, dst_ref=dst, send_sem=ss.at[to], recv_sem=rs.at[frm],
            device_id={"blk": to}, device_id_type=MESH,
        )

    def peers(body):
        def step(i, _):
            body(lax.rem(me + i, n))
            return 0

        lax.fori_loop(1, n, step, 0)

    def blk_peers(body):
        for i in range(1, nb):
            body(lax.rem(mb + i, nb))

    sid = span_id[...]
    mine = table[:, 0:negatives]
    for h in range(1, own_rows // negatives):
        mine = jnp.where(sid == h, table[:, h * negatives:(h + 1) * negatives], mine)
    spans[mb] = mine

    def send_span(c):
        to_blk(spans.at[mb], spans.at[mb], span_ss, span_rs, c, mb).start()

    blk_peers(send_span)

    def ask(q):
        acc = jnp.zeros((wanted.shape[0], cap), F32)
        for e in range(0, 2 * edges, chunk):
            pick = onehot(cap, q * cap, slots[:, e:e + chunk])
            acc = acc + dot(wanted[:, e:e + chunk], pick, NT)
        return acc[0:8]

    def send_ask(q):
        req_out[q] = ask(q)
        to_shard(req_out.at[q], req_in.at[me], req_ss, req_rs, q, me).start()

    peers(send_ask)
    req_in[me] = ask(me)

    def asked(q):
        both = req_in[q]
        return (both[0:1] * 256.0 + both[1:2]).astype(jnp.int32)

    def look_up(q):
        ids = asked(q)
        acc = jnp.zeros((width, cap), F32)
        for r in range(0, own_rows, chunk):
            acc = acc + dot(table[:, r:r + chunk], onehot(chunk, r, ids), NN)
        return acc.astype(BF)

    def send_rows(q):
        to_shard(req_out.at[q], req_in.at[q], req_ss, req_rs, q, q).wait_recv()
        row_out[q] = look_up(q)
        to_shard(row_out.at[q], row_in.at[me], row_ss, row_rs, q, me).start()

    peers(send_rows)
    row_in[me] = look_up(me)

    rel_pad[...] = jnp.zeros(rel_pad.shape, BF)
    rel_pad[:, 0:types] = relation[...]
    for e in range(0, edges, chunk):
        acc = jnp.zeros((width, chunk), F32)
        for r in range(0, rel_pad.shape[1], part):
            acc = acc + dot(rel_pad[:, r:r + part], onehot(part, r, rel_ids[:, e:e + chunk]), NN)
        rel_rows[:, e:e + chunk] = acc

    def place(q, first):
        rows = row_in[q]
        for e in range(0, 2 * edges, chunk):
            add = dot(rows, onehot(cap, q * cap, slots[:, e:e + chunk]), NN)
            if first:
                ends[:, e:e + chunk] = add
            else:
                ends[:, e:e + chunk] += add

    place(me, True)

    def take_rows(q):
        to_shard(row_out.at[q], row_in.at[q], row_ss, row_rs, q, q).wait_recv()
        place(q, False)

    peers(take_rows)

    block = 128

    def query_step(j, _):
        at = pl.ds(pl.multiple_of(j * block, block), block)
        at_target = pl.ds(pl.multiple_of(edges + j * block, block), block)
        s_re, s_im = ends[0:half, at], ends[half:width, at]
        r_re, r_im = rel_rows[0:half, at], rel_rows[half:width, at]
        t_re, t_im = ends[0:half, at_target], ends[half:width, at_target]
        a = s_re * r_re - s_im * r_im
        b = s_re * r_im + s_im * r_re
        score = jnp.sum(a * t_re, axis=0, keepdims=True) + jnp.sum(b * t_im, axis=0, keepdims=True)
        pos = jax.nn.sigmoid(score) - 1.0
        query_s[0:half, at] = a
        query_s[half:width, at] = b
        query_grad[0:half, at] = pos * t_re
        query_grad[half:width, at] = pos * t_im
        end_grads[:, at_target] = (pos * query_s[:, at]).astype(BF)
        query_bf[:, at] = query_s[:, at].astype(BF)
        return 0

    lax.fori_loop(0, edges // block, query_step, 0)

    tile = 256

    def visit(c, own):
        def step(j, _):
            at = pl.ds(pl.multiple_of(j * tile, tile), tile)
            sp = spans[c, :, at]
            score = dot(sp, query_bf[...], TN)
            g = (weight * jax.nn.sigmoid(score)).astype(BF)
            query_grad[...] += dot(sp, g, NN)
            term = dot(query_bf[...], g, NT)
            if own:
                own_back[:, at] = term
            else:
                back_out[c, :, at] = term.astype(BF)
            return 0

        lax.fori_loop(0, negatives // tile, step, 0)

    def peer_visit(i, _):
        c = lax.rem(mb + i, nb)
        to_blk(spans.at[c], spans.at[c], span_ss, span_rs, c, c).wait_recv()
        visit(c, False)
        to_blk(back_out.at[c], back_in.at[mb], back_ss, back_rs, c, mb).start()
        return 0

    lax.fori_loop(1, nb, peer_visit, 0)
    visit(mb, True)

    def grad_step(j, _):
        at = pl.ds(pl.multiple_of(j * block, block), block)
        s_re, s_im = ends[0:half, at], ends[half:width, at]
        r_re, r_im = rel_rows[0:half, at], rel_rows[half:width, at]
        q_re, q_im = query_grad[0:half, at], query_grad[half:width, at]
        query_s[0:half, at] = q_re * r_re + q_im * r_im
        query_s[half:width, at] = q_im * r_re - q_re * r_im
        end_grads[:, at] = query_s[:, at].astype(BF)
        rel_rows[0:half, at] = q_re * s_re + q_im * s_im
        rel_rows[half:width, at] = q_im * s_re - q_re * s_im
        term = rel_rows[:, at]
        hi = term.astype(BF)
        rel_hi[:, at] = hi
        rel_lo[:, at] = (term - hi.astype(F32)).astype(BF)
        return 0

    lax.fori_loop(0, edges // block, grad_step, 0)

    def rel_sum(c):
        acc = jnp.zeros((width, part), F32)
        for e in range(0, edges, chunk):
            pick = onehot(part, c * part, rel_ids[:, e:e + chunk])
            acc = acc + dot(rel_hi[:, e:e + chunk], pick, NT)
            acc = acc + dot(rel_lo[:, e:e + chunk], pick, NT)
        return acc

    def send_rel(i, _):
        c = lax.rem(mb + i, nb)
        r1_out[c] = rel_sum(c)
        to_blk(r1_out.at[c], r1_in.at[mb], r1_ss, r1_rs, c, mb).start()
        return 0

    lax.fori_loop(1, nb, send_rel, 0)

    def collect(q):
        acc = jnp.zeros((width, cap), F32)
        for e in range(0, 2 * edges, chunk):
            pick = onehot(cap, q * cap, slots[:, e:e + chunk])
            acc = acc + dot(end_grads[:, e:e + chunk], pick, NT)
        return acc.astype(BF)

    def send_grads(q):
        to_shard(row_out.at[q], row_in.at[me], row_ss, row_rs, q, me).wait_send()
        grad_out[q] = collect(q)
        to_shard(grad_out.at[q], grad_in.at[me], grad_ss, grad_rs, q, me).start()

    peers(send_grads)
    grad_in[me] = collect(me)
    r1_in[mb] = rel_sum(mb)

    def settle(q, first):
        ids = asked(q)
        got = grad_in[q]
        for r in range(0, own_rows, chunk):
            add = dot(got, onehot(chunk, r, ids), NT)
            if first:
                entity[:, r:r + chunk] = add
            else:
                entity[:, r:r + chunk] += add

    def take_r1(c):
        to_blk(r1_out.at[c], r1_in.at[c], r1_ss, r1_rs, c, c).wait_recv()

    blk_peers(take_r1)
    total = r1_in[0]
    for c in range(1, nb):
        total = total + r1_in[c]
    r2_out[...] = jnp.zeros(r2_out.shape, BF)
    r2_out[0:width] = total.astype(BF)

    def piece_at(q):
        return pl.ds(pl.multiple_of(q * piece, piece), piece)

    def send_r2(q):
        to_shard(r2_out.at[piece_at(q)], r2_in.at[me], r2_ss, r2_rs, q, me).start()

    peers(send_r2)
    r2_in[me] = r2_out[piece_at(me)]
    settle(me, True)

    def take_r2(q):
        to_shard(r2_out.at[piece_at(q)], r2_in.at[q], r2_ss, r2_rs, q, q).wait_recv()

    peers(take_r2)

    def add_r2(q, acc):
        return acc + r2_in[q].astype(F32)

    r3[piece_at(me)] = lax.fori_loop(0, n, add_r2, jnp.zeros((piece, part), F32))

    def send_r3(q):
        to_shard(r3.at[piece_at(me)], r3.at[piece_at(me)], r3_ss, r3_rs, q, me).start()

    peers(send_r3)

    def take_r3(q):
        to_shard(r3.at[piece_at(q)], r3.at[piece_at(q)], r3_ss, r3_rs, q, q).wait_recv()

    peers(take_r3)
    whole = r3.at[pl.ds(0, width)]

    def send_r4(c):
        to_blk(whole, r4_in.at[mb], r4_ss, r4_rs, c, mb).start()

    blk_peers(send_r4)
    r4_in[mb] = r3[0:width]

    def take_grads(q):
        to_shard(grad_out.at[q], grad_in.at[q], grad_ss, grad_rs, q, q).wait_recv()
        settle(q, False)

    peers(take_grads)

    def take_back(c):
        to_blk(back_out.at[c], back_in.at[c], back_ss, back_rs, c, c).wait_recv()
        own_back[...] += back_in[c].astype(F32)

    blk_peers(take_back)
    for h in range(own_rows // negatives):
        entity[:, h * negatives:(h + 1) * negatives] += jnp.where(sid == h, own_back[...], 0.0)

    def take_r4(c):
        to_blk(whole, r4_in.at[c], r4_ss, r4_rs, c, c).wait_recv()

    blk_peers(take_r4)
    for c in range(nb):
        wide = min(part, types - c * part)
        if wide > 0:
            relation_out[:, c * part:c * part + wide] = r4_in[c][:, 0:wide]

    def finish(q):
        to_shard(req_out.at[q], req_in.at[me], req_ss, req_rs, q, me).wait_send()
        to_shard(grad_out.at[q], grad_in.at[me], grad_ss, grad_rs, q, me).wait_send()
        to_shard(r2_out.at[piece_at(q)], r2_in.at[me], r2_ss, r2_rs, q, me).wait_send()
        to_shard(r3.at[piece_at(me)], r3.at[piece_at(me)], r3_ss, r3_rs, q, me).wait_send()

    peers(finish)

    def finish_blk(c):
        to_blk(spans.at[mb], spans.at[mb], span_ss, span_rs, c, mb).wait_send()
        to_blk(back_out.at[c], back_in.at[mb], back_ss, back_rs, c, mb).wait_send()
        to_blk(r1_out.at[c], r1_in.at[mb], r1_ss, r1_rs, c, mb).wait_send()
        to_blk(whole, r4_in.at[mb], r4_ss, r4_rs, c, mb).wait_send()

    blk_peers(finish_blk)


def round_up(a, b):
    return -(-a // b) * b


def shards(table, relation, owners, rows, rel_ids, span_ids):
    n = lax.axis_size("shard")
    nb = lax.axis_size("blk")
    edges = owners.shape[0]
    own_rows, width = table.shape
    types = relation.shape[0]
    cap = 4 * edges // n
    part = round_up(-(-types // nb), 128)
    piece = round_up(-(-width // n), 16)
    flat_owner = owners.T.reshape(-1)
    flat_row = rows.T.reshape(-1)
    hot = (flat_owner[None, :] == jnp.arange(n, dtype=jnp.int32)[:, None]).astype(jnp.int32)
    ranking = jnp.sum(jnp.cumsum(hot, axis=1) * hot, axis=0) - 1
    slots = (flat_owner * cap + ranking).reshape(1, 2 * edges)
    wanted = jnp.concatenate(
        [(flat_row // 256)[None], (flat_row % 256)[None], jnp.zeros((14, 2 * edges), jnp.int32)]
    ).astype(BF)

    vm = pltpu.VMEM
    dma = pltpu.SemaphoreType.DMA
    scratch = [
        vm((n, 8, cap), F32), vm((n, 8, cap), F32),
        vm((n, width, cap), BF), vm((n, width, cap), BF), vm((n, width, cap), BF),
        vm((nb, width, NEG), BF), vm((nb, width, NEG), BF), vm((nb, width, NEG), BF),
        vm((width, NEG), F32),
        vm((width, nb * part), BF), vm((width, edges), F32),
        vm((width, edges), F32), vm((width, edges), BF), vm((width, edges), F32),
        vm((width, 2 * edges), BF), vm((width, edges), BF),
        vm((nb, width, part), F32), vm((nb, width, part), F32),
        vm((n * piece, part), BF), vm((n, piece, part), BF), vm((n * piece, part), F32),
        vm((nb, width, part), F32),
    ]
    scratch += [dma((n,))] * 6 + [dma((nb,))] * 6 + [dma((n,))] * 4 + [dma((nb,))] * 2
    spec = pl.BlockSpec(memory_space=pltpu.VMEM)
    entity, rel_grad = pl.pallas_call(
        functools.partial(kernel, n, nb, cap, piece),
        out_shape=(
            jax.ShapeDtypeStruct((width, own_rows), F32),
            jax.ShapeDtypeStruct((width, types), F32),
        ),
        in_specs=[spec] * 6,
        out_specs=(spec, spec),
        scratch_shapes=scratch,
        compiler_params=pltpu.CompilerParams(
            collective_id=0, has_side_effects=True, vmem_limit_bytes=60 * 1024 * 1024
        ),
    )(table.T, relation.T, slots, wanted, rel_ids.reshape(1, edges), span_ids.reshape(1, 1))
    return (entity.T, rel_grad.T)


def solution(mesh):
    in_specs = (
        P(("blk", "shard"), None),
        P(),
        P(("blk", "shard"), None),
        P(("blk", "shard"), None),
        P(("blk", "shard")),
        P(("blk", "shard")),
    )
    out_specs = (P(("blk", "shard"), None), P())
    return jax.shard_map(shards, mesh=mesh, in_specs=in_specs, out_specs=out_specs, check_vma=False)
```

time: 577 us -> 258 us (0.45); the launches traced: 566 us -> 257 us
  waiting for transfers between devices: 310 us -> 0 us
  Pallas kernels: 0 us -> 244 us
  local copies, waits for them, and re-layouts: 137 us -> 7.33 us
  other arithmetic: 53.5 us -> 4.63 us
  matrix products: 24.7 us -> 0 us
  starting transfers between devices: 24 us -> 0 us
  between operations: 15.8 us -> 1.34 us
    pallas_call x0 -> x1, Pallas kernels: none -> 244 us  [shards(): pl.pallas_call(functools.partial(kernel, n, nb, cap, piece), out_shape=(j...]
    psum x1 -> x0, waiting for transfers between devices: 140 us -> none  [shards(): relation_grad = lax.psum(local_relation, ('blk', 'shard'))]
    ppermute x7 -> x0, waiting for transfers between devices: 139 us -> none  [from_behind(): lax.ppermute(value, axis, [(i, (i + by) % length) for i in range(length)])]
    gather x5 -> x0, local copies, waits for them, and re-layouts: 39.9 us -> none  [the longest x2 23.5 us: shards(): table[asked_rows]]
    scatter-add x2 -> x0, other arithmetic: 39.3 us -> none  [the longest x1 30.4 us: shards(): entity_grad = jnp.zeros((rows_own, width), jnp.float32).at[asked_rows.res...]
    all_to_all x3 -> x0, waiting for transfers between devices: 30.8 us -> none  [the longest x1 29.6 us: shards(): lax.all_to_all(table[asked_rows], 'shard', split_axis=0, concat_axis=0, t...]
    reshape x5 -> x0, local copies, waits for them, and re-layouts: 26.3 us -> none  [the longest x1 8.53 us: shards(): arrived.reshape(-1, width)]
    dot_general x12 -> x0, matrix products: 24.7 us -> none  [the longest x4 12.3 us: score_span(): lax.dot_general(query_bf, span, (((1,), (1,)), ((), ())), preferred_eleme...]
  transfers between devices with their start and end apart: 11 -> 0, of which waited for: 8 -> 0; matrix products, arithmetic and copies ran while one was open for 21% -> 0% of each run, Pallas kernels for 0% -> 0%
where the time goes in v1:
time: 258 us; the launch traced here: 257 us
  Pallas kernels  244 us (95%)
  local copies, waits for them, and re-layouts  7.33 us (3%)
  other arithmetic  4.63 us (2%)
    pallas_call x1, Pallas kernels, shards(): pl.pallas_call(functools.partial(kernel, n, nb, cap, piece), out_shape=(j...  244 us
    unnamed x6, local copies, waits for them, and re-layouts  6.25 us

profile of v1, /device:TPU:9, one launch (start us, length us, event | category | flops | bytes accessed | tf_op | source)
XLA Modules:
  0.0 257.2 jit_solution(9548594037277155449)
XLA Ops:
  1.3 0.1 pad.2.clone
  1.4 0.7 eq.19
  2.1 0.7 copy.9
  2.8 0.7 multiply_bitcast_fusion
  3.6 0.7 maximum_maximum_fusion.wanted
  4.3 2.3 reduce-window.6
  6.6 0.3 slice_reduce_fusion
  6.9 0.2 reduce-window.9
  7.0 0.1 select_reduce_fusion
  7.1 0.6 add.40.slots
  7.7 243.9 %shard_map.77 = (f32[400,2048]{1,0:T(8,128)}, f32[400,1345]{1,0:T(8,128)}) custom-call(bf16[400,2048]{1,0:T(8,128)(2,1)} %bitcast.21, bf16[400,1345]{1,0:T(8,128)(2,1)} %bitcast.22, s32[1,2048]{1,0:T(1,128)} %add.40.slots, bf16[16,2048]{1,0:T(8,128)(2,1)} %maximum_maximum_fusion.wanted, s32[1,1024]{1,0:T(1,128)} %bitcast.29, s32[1,1]{1,0:T(1,128)} %bitcast.18.span_id), custom_call_target="tpu_custom_call" | custom-call | tf_op jit(solution)/shard_map/pallas_call | solution.py:393
  251.6 0.0 copy-start
  251.6 4.2 %copy.13 = f32[2048,400]{0,1:T(8,128)} copy(f32[2048,400]{0,1:T(8,128)} %bitcast.19) | data formatting | bytes 6553600
  255.8 0.0 copy-done
  255.8 1.4 copy.14
  (6 shorter events, 0.1 us)
Async XLA Ops:
  251.6 4.2 %copy-start = (f32[400,1345]{1,0:T(8,128)S(1)}, f32[400,1345]{1,0:T(8,128)}, u32[]{:S(2)}) copy-start(f32[400,1345]{1,0:T(8,128)} %get-tuple-element.5) | copy-start | bytes 6456004

commit v2 on v1

--- a/solution.py
+++ b/solution.py
@@ -75,12 +75,19 @@
             device_id={"blk": to}, device_id_type=MESH,
         )
 
-    def peers(body):
+    def peers(body, first=1, last=n):
         def step(i, _):
             body(lax.rem(me + i, n))
             return 0
 
-        lax.fori_loop(1, n, step, 0)
+        lax.fori_loop(first, last, step, 0)
+
+    def senders(body, first=1, last=n):
+        def step(i, _):
+            body(lax.rem(me + n - i, n))
+            return 0
+
+        lax.fori_loop(first, last, step, 0)
 
     def blk_peers(body):
         for i in range(1, nb):
@@ -153,7 +160,7 @@
         to_shard(row_out.at[q], row_in.at[q], row_ss, row_rs, q, q).wait_recv()
         place(q, False)
 
-    peers(take_rows)
+    senders(take_rows)
 
     block = 128
 
@@ -196,14 +203,13 @@
         lax.fori_loop(0, negatives // tile, step, 0)
 
     def peer_visit(i, _):
-        c = lax.rem(mb + i, nb)
+        c = lax.rem(mb + nb - i, nb)
         to_blk(spans.at[c], spans.at[c], span_ss, span_rs, c, c).wait_recv()
         visit(c, False)
-        to_blk(back_out.at[c], back_in.at[mb], back_ss, back_rs, c, mb).start()
         return 0
 
+    visit(mb, True)
     lax.fori_loop(1, nb, peer_visit, 0)
-    visit(mb, True)
 
     def grad_step(j, _):
         at = pl.ds(pl.multiple_of(j * block, block), block)
@@ -239,6 +245,11 @@
 
     lax.fori_loop(1, nb, send_rel, 0)
 
+    def send_back(c):
+        to_blk(back_out.at[c], back_in.at[mb], back_ss, back_rs, c, mb).start()
+
+    blk_peers(send_back)
+
     def collect(q):
         acc = jnp.zeros((width, cap), F32)
         for e in range(0, 2 * edges, chunk):
@@ -251,7 +262,9 @@
         grad_out[q] = collect(q)
         to_shard(grad_out.at[q], grad_in.at[me], grad_ss, grad_rs, q, me).start()
 
-    peers(send_grads)
+    lot_1 = 1 + n // 2
+    lot_2 = n - max(1, n // 8)
+    peers(send_grads, 1, lot_1)
     grad_in[me] = collect(me)
     r1_in[mb] = rel_sum(mb)
 
@@ -282,6 +295,7 @@
         to_shard(r2_out.at[piece_at(q)], r2_in.at[me], r2_ss, r2_rs, q, me).start()
 
     peers(send_r2)
+    peers(send_grads, lot_1, lot_2)
     r2_in[me] = r2_out[piece_at(me)]
     settle(me, True)
 
@@ -299,24 +313,27 @@
         to_shard(r3.at[piece_at(me)], r3.at[piece_at(me)], r3_ss, r3_rs, q, me).start()
 
     peers(send_r3)
-
-    def take_r3(q):
-        to_shard(r3.at[piece_at(q)], r3.at[piece_at(q)], r3_ss, r3_rs, q, q).wait_recv()
-
-    peers(take_r3)
-    whole = r3.at[pl.ds(0, width)]
-
-    def send_r4(c):
-        to_blk(whole, r4_in.at[mb], r4_ss, r4_rs, c, mb).start()
-
-    blk_peers(send_r4)
-    r4_in[mb] = r3[0:width]
+    peers(send_grads, lot_2, n)
 
     def take_grads(q):
         to_shard(grad_out.at[q], grad_in.at[q], grad_ss, grad_rs, q, q).wait_recv()
         settle(q, False)
 
-    peers(take_grads)
+    senders(take_grads, 1, lot_1)
+
+    def take_r3(q):
+        to_shard(r3.at[piece_at(q)], r3.at[piece_at(q)], r3_ss, r3_rs, q, q).wait_recv()
+
+    peers(take_r3)
+    whole = r3.at[pl.ds(0, width)]
+
+    def send_r4(c):
+        to_blk(whole, r4_in.at[mb], r4_ss, r4_rs, c, mb).start()
+
+    blk_peers(send_r4)
+    r4_in[mb] = r3[0:width]
+
+    senders(take_grads, lot_1, n)
 
     def take_back(c):
         to_blk(back_out.at[c], back_in.at[c], back_ss, back_rs, c, c).wait_recv()

time: 258 us -> 257 us (level)
  no operation moved by 1% of the time
where the time goes in v2:
time: 257 us
  Pallas kernels  243 us (95%)
  local copies, waits for them, and re-layouts  7.33 us (3%)
  other arithmetic  4.63 us (2%)
    pallas_call x1, Pallas kernels, shards(): pl.pallas_call(functools.partial(kernel, n, nb, cap, piece), out_shape=(j...  243 us
    unnamed x6, local copies, waits for them, and re-layouts  6.25 us

profile of v2, /device:TPU:9, one launch (start us, length us, event | category | flops | bytes accessed | tf_op | source)
XLA Modules:
  0.0 256.6 jit_solution(4842745835528642152)
XLA Ops:
  1.3 0.1 pad.2.clone
  1.4 0.7 eq.19
  2.1 0.7 copy.9
  2.8 0.7 multiply_bitcast_fusion
  3.6 0.7 maximum_maximum_fusion.wanted
  4.3 2.3 reduce-window.6
  6.6 0.3 slice_reduce_fusion
  6.9 0.2 reduce-window.9
  7.0 0.1 select_reduce_fusion
  7.1 0.6 add.40.slots
  7.7 243.3 %shard_map.77 = (f32[400,2048]{1,0:T(8,128)}, f32[400,1345]{1,0:T(8,128)}) custom-call(bf16[400,2048]{1,0:T(8,128)(2,1)} %bitcast.21, bf16[400,1345]{1,0:T(8,128)(2,1)} %bitcast.22, s32[1,2048]{1,0:T(1,128)} %add.40.slots, bf16[16,2048]{1,0:T(8,128)(2,1)} %maximum_maximum_fusion.wanted, s32[1,1024]{1,0:T(1,128)} %bitcast.29, s32[1,1]{1,0:T(1,128)} %bitcast.18.span_id), custom_call_target="tpu_custom_call" | custom-call | tf_op jit(solution)/shard_map/pallas_call | solution.py:410
  251.1 0.0 copy-start
  251.1 4.2 %copy.13 = f32[2048,400]{0,1:T(8,128)} copy(f32[2048,400]{0,1:T(8,128)} %bitcast.19) | data formatting | bytes 6553600
  255.2 0.0 copy-done
  255.2 1.4 copy.14
  (6 shorter events, 0.1 us)
Async XLA Ops:
  251.1 4.2 %copy-start = (f32[400,1345]{1,0:T(8,128)S(1)}, f32[400,1345]{1,0:T(8,128)}, u32[]{:S(2)}) copy-start(f32[400,1345]{1,0:T(8,128)} %get-tuple-element.5) | copy-start | bytes 6456004
